TPU v7x, 128 devices: a whole 4x4x4 slice. The times are simulated.
128 devices in a mesh: roll: 32 (over z, x, y_lo), tp: 4 (over y_hi, core).
Axes of the slice: x: 4, y: 4 (y_hi: 2, y_lo: 2; y = y_hi * 2 + y_lo), z: 4, core: 2. Of those that a mesh axis runs over, the one named last changes fastest.
Arguments:
- prompt_states: bfloat16 [4, 8192, 8192], P(None, 'roll'), may hold values from -1500 to 1500
- decode_states: bfloat16 [1024, 8192], P(None, 'roll'), may hold values from -1500 to 1500
- norm_gain: bfloat16 [8192], replicated, may hold values from 0.5 to 1.5
- latent_down: bfloat16 [8192, 2048], P(None, 'tp')
- key_up: bfloat16 [8, 256, 128], P('tp')
- value_up: bfloat16 [8, 256, 128], P('tp'), may hold values from -0.375 to 0.375
- query_weight: bfloat16 [8192, 8192], P('roll', 'tp')
- out_weight: bfloat16 [8192, 8192], P('tp', 'roll'), may hold values from -0.0625 to 0.0625
- prompt_lengths: int32 [4], replicated, may hold values from 4096 to 8192, as said below
- group_prompt: int32 [32], replicated, may hold values from 0 to 3
Outputs:
- attn_out: bfloat16 [1024, 8192], P('tp', 'roll')
Inputs may be any that keep to these rules, and one draw needn't show every extreme that they name: `prompt_lengths`: some prompt has all 8192 tokens valid.
All inputs are finite; a program needn't handle non-finite values.
Results may differ from a plain program's by a relative error of at most 0.035.
Values may be sent and summed in bfloat16 or wider, within the bound.
A program may use at most 192 MiB of HBM per device.

v0:
```python
import jax
import jax.numpy as jnp
from jax import lax
from jax.sharding import PartitionSpec as P

HD = 128
RANK = 256
STEPS = 4


eps = 1e-06
rope_base = 1000000.0


def rotate(values, positions):
    half_dim = values.shape[-1] // 2
    inverse_freq = rope_base ** (
        -(jnp.arange(half_dim, dtype=jnp.float32) * 2.0 / values.shape[-1])
    )
    angles = positions[..., None].astype(jnp.float32) * inverse_freq
    cosine = jnp.cos(angles)
    sines = jnp.sin(angles)
    front_half = values[..., :half_dim]
    back_half = values[..., half_dim:]
    return jnp.concatenate(
        [front_half * cosine - back_half * sines, back_half * cosine + front_half * sines], axis=-1
    )


def local(
    prompt_states,
    decode_states,
    norm_gain,
    latent_down,
    key_up,
    value_up,
    query_weight,
    out_weight,
    prompt_lengths,
    group_prompt,
):
    group_total = lax.axis_size("roll")
    roll_index = lax.axis_index("roll")
    model_width = norm_gain.shape[0]
    slab_width = decode_states.shape[1]
    rows_all = decode_states.shape[0]
    rows_mine = rows_all // group_total
    head_count = query_weight.shape[1] // HD
    group_count = key_up.shape[0]
    per_group = head_count // group_count
    gain_full = norm_gain.astype(jnp.float32)
    gain_slab = lax.dynamic_slice_in_dim(gain_full, roll_index * slab_width, slab_width)
    down_slab = lax.dynamic_slice_in_dim(latent_down, roll_index * slab_width, slab_width, 0)
    widened = decode_states.astype(jnp.float32)
    squares = jnp.sum(widened * widened, axis=1)
    scaled_rows = (widened * gain_slab).astype(jnp.bfloat16)
    joined_weight = jnp.concatenate([query_weight, down_slab], axis=1)
    total_squares = lax.psum(squares, "roll")
    own_squares = lax.dynamic_slice_in_dim(total_squares, roll_index * rows_mine, rows_mine)
    projected = lax.psum_scatter(
        jnp.dot(scaled_rows, joined_weight, preferred_element_type=jnp.float32).astype(
            jnp.bfloat16
        ),
        "roll",
        scatter_dimension=0,
        tiled=True,
    ).astype(jnp.float32)
    inverse_rms = lax.rsqrt(own_squares / model_width + eps)
    query_raw = inverse_rms[:, None] * projected[:, : head_count * HD]
    decode_latent = (inverse_rms[:, None] * projected[:, head_count * HD :]).astype(jnp.bfloat16)
    decode_latent = decode_latent.reshape(rows_mine, group_count, RANK)
    prompt = group_prompt[roll_index]
    length = prompt_lengths[prompt]
    row_index = jnp.arange(rows_mine, dtype=jnp.int32)
    positions = length + row_index % STEPS
    queries = rotate(query_raw.reshape(rows_mine, head_count, HD), positions[:, None]).astype(
        jnp.bfloat16
    )
    queries = queries.reshape(rows_mine, group_count, per_group, HD)
    rebuilt = jnp.einsum("nkr,krd->nkd", decode_latent, key_up, preferred_element_type=jnp.float32)
    decode_keys = rotate(rebuilt, positions[:, None]).astype(jnp.bfloat16)
    scaling = HD ** (-0.5)
    allowed = (row_index[:, None] // STEPS == row_index[None, :] // STEPS) & (
        row_index[None, :] <= row_index[:, None]
    )
    self_scores = (
        jnp.einsum("rkhd,nkd->rkhn", queries, decode_keys, preferred_element_type=jnp.float32)
        * scaling
    )
    self_scores = jnp.where(allowed[:, None, None, :], self_scores, -jnp.inf)
    running_max = jnp.max(self_scores, axis=-1)
    weights_raw = jnp.exp(self_scores - running_max[..., None])
    run_total = jnp.sum(weights_raw, axis=-1)
    latent_sum = jnp.einsum(
        "rkhn,nkc->rkhc",
        weights_raw.astype(jnp.bfloat16),
        decode_latent,
        preferred_element_type=jnp.float32,
    )
    widened_prompts = prompt_states.astype(jnp.float32)
    prompt_rms = lax.rsqrt(
        jnp.mean(widened_prompts * widened_prompts, axis=-1, keepdims=True) + eps
    )
    prompt_normed = (widened_prompts * prompt_rms * gain_full).astype(jnp.bfloat16)
    latent_pages = jnp.dot(prompt_normed, latent_down, preferred_element_type=jnp.float32).astype(
        jnp.bfloat16
    )
    selected = lax.dynamic_index_in_dim(
        lax.all_gather(latent_pages, "roll", axis=1, tiled=True), prompt, 0, keepdims=False
    )
    latent_block = selected
    block_size = latent_block.shape[0]
    latent_block = latent_block.reshape(block_size, group_count, RANK)
    key_spots = jnp.arange(block_size, dtype=jnp.int32)
    block_keys = jnp.einsum(
        "nkr,krd->nkd", latent_block, key_up, preferred_element_type=jnp.float32
    )
    block_keys = rotate(block_keys, key_spots[:, None]).astype(jnp.bfloat16)
    far_scores = (
        jnp.einsum("rkhd,nkd->rkhn", queries, block_keys, preferred_element_type=jnp.float32)
        * scaling
    )
    far_scores = jnp.where(key_spots < length, far_scores, -jnp.inf)
    new_max = jnp.maximum(running_max, jnp.max(far_scores, axis=-1))
    rescale = jnp.exp(running_max - new_max)
    block_weights = jnp.exp(far_scores - new_max[..., None])
    new_total = run_total * rescale + jnp.sum(block_weights, axis=-1)
    new_sum = latent_sum * rescale[..., None] + jnp.einsum(
        "rkhn,nkc->rkhc",
        block_weights.astype(jnp.bfloat16),
        latent_block,
        preferred_element_type=jnp.float32,
    )
    finished = (new_max, new_total, new_sum)
    final_max, final_total, final_sum = finished
    latent_mix = (final_sum / final_total[..., None]).astype(jnp.bfloat16)
    head_values = jnp.einsum(
        "rkhc,kcd->rkhd", latent_mix, value_up, preferred_element_type=jnp.float32
    ).astype(jnp.bfloat16)
    head_values = head_values.reshape(rows_mine, head_count * HD)
    partial_value = jnp.dot(
        lax.all_gather(head_values, "roll", axis=0, tiled=True),
        out_weight,
        preferred_element_type=jnp.float32,
    )
    return lax.psum_scatter(
        partial_value.astype(jnp.bfloat16), "tp", scatter_dimension=0, tiled=True
    )


def solution(mesh):
    return jax.shard_map(
        local,
        mesh=mesh,
        in_specs=(
            P(None, "roll", None),
            P(None, "roll"),
            P(),
            P(None, "tp"),
            P("tp", None, None),
            P("tp", None, None),
            P("roll", "tp"),
            P("tp", "roll"),
            P(),
            P(),
        ),
        out_specs=P("tp", "roll"),
        check_vma=False,
    )
```

profile of v0, /device:TPU:1, one launch (start us, length us, event | category | flops | bytes accessed | tf_op | source)
XLA Modules:
  0.0 1152.9 jit_solution(15181876154769069208)
XLA Ops:
  6.5 0.0 copy-start
  6.5 0.0 reduce-scatter.3.cloned.1.call-start
  6.5 1.1 constant_dynamic-slice_fusion.1
  7.6 0.8 dynamic_slice.20
  8.4 5.3 convolution_convert_fusion
  13.7 0.0 reduce-scatter.3.cloned.1.call-update
  13.7 0.0 all-gather.3.cloned.1.call-start
  13.7 0.0 copy-done.8
  13.8 7.2 fusion
  21.0 0.0 copy-start.11
  21.0 0.0 copy-start.12
  21.0 0.0 copy-start.2
  21.0 15.9 %fusion.16 = bf16[4,256,512]{2,1,0:T(8,128)(2,1)} fusion(bf16[8192,512]{1,0:T(8,128)(2,1)} %param.13, bf16[4,256,8192]{2,1,0:T(8,128)(2,1)} %param.10, f32[8192]{0:T(1024)S(1)} %convert_element_type.73, f32[4,256]{1,0:T(4,128)S(1)} %add_rsqrt_fusion), kind=kOutput, calls=%fused_computation.27 | convolution fusion | flops 8624013312 | bytes 26251264 | tf_op jit(solution)/shard_map/dot_general | solution.py:105
  36.9 0.0 all-gather.3.cloned.1.call-update
  36.9 0.0 all-gather.5.cloned.1.call-start
  37.0 0.0 copy-done.11
  37.0 0.6 dynamic_slice.22
  39.5 0.0 copy-done.12
  39.5 0.6 dynamic_slice.23
  40.1 0.0 copy-done.2
  40.1 0.2 fusion.36
  40.3 74.4 %psum.7 = f32[1024]{0:T(1024)S(1)} all-reduce(f32[1024]{0:T(1024)S(1)} %fusion.36), channel_id=1, replica_groups=mesh['roll'=32,'tp'=4] {'roll'}, use_global_device_ids=true, to_apply=%region_1.0 | all-reduce | flops 1024 | bytes 8192 | tf_op jit(solution)/shard_map/psum | solution.py:58
  114.8 0.1 add_rsqrt_fusion.1
  114.8 0.7 and_select_fusion.1
  115.5 1.2 iota_compare_fusion
  116.8 0.7 fusion.53
  117.4 0.1 multiply_cosine_fusion.1
  117.6 0.0 copy-start.4
  117.6 8.4 multiply_cosine_fusion
  126.0 40.1 %reduce-scatter.3.cloned.1.call-done = bf16[32,2560]{1,0:T(8,128)(2,1)} async-done(((bf16[1024,2560]{1,0:T(8,128)(2,1)}), bf16[32,2560]{1,0:T(8,128)(2,1)}) %reduce-scatter.3.cloned.1.call-update) | async-done | bytes 163856 | tf_op jit(solution)/shard_map/reduce_scatter | solution.py:60
  166.1 0.9 convert_element_type.76
  167.0 0.1 fusion.40
  167.1 0.2 subtract_convert_fusion.1
  167.3 0.0 copy-done.9
  167.4 1.3 fusion.46
  168.7 1.4 reshape.304
  170.1 0.0 copy-done.3
  170.1 0.9 convolution_bitcast_fusion.2
  171.0 0.8 subtract_convert_fusion.2
  171.8 1.1 fusion.59
  172.9 0.7 fusion.43
  173.6 1.7 copy.30
  175.3 720.9 %all-gather.3.cloned.1.call-done = bf16[4,8192,512]{2,1,0:T(8,128)(2,1)} async-done(((bf16[4,256,512]{2,1,0:T(8,128)(2,1)}), bf16[4,8192,512]{2,1,0:T(8,128)(2,1)}) %all-gather.3.cloned.1.call-update) | async-done | bytes 33554448 | tf_op jit(solution)/shard_map/all_gather | solution.py:109
  896.2 7.1 constant_dynamic-slice_fusion
  903.3 11.3 copy.21
  914.6 4.8 convolution_bitcast_fusion
  919.5 2.5 subtract_convert_fusion
  922.0 0.0 copy-done.6
  922.0 4.9 bitcast_reduce_fusion
  926.9 6.5 fusion.8
  933.4 0.1 copy.26
  933.5 0.1 copy.25
  933.5 0.0 copy-start.5
  933.6 0.0 copy-start.7
  933.6 0.0 copy-start.10
  933.6 11.3 fusion.27
  944.9 0.4 fusion.35
  945.3 0.7 copy.54
  946.0 0.0 all-gather.5.cloned.1.call-update
  946.1 0.0 reduce-scatter.5.cloned.1.call-start
  946.1 147.9 %all-gather.5.cloned.1.call-done = bf16[1024,2048]{1,0:T(8,128)(2,1)} async-done(((bf16[32,2048]{1,0:T(8,128)(2,1)}), bf16[1024,2048]{1,0:T(8,128)(2,1)}) %all-gather.5.cloned.1.call-update) | async-done | bytes 4194320 | tf_op jit(solution)/shard_map/all_gather | solution.py:142
  1094.0 4.2 convolution_convert_fusion.1
  1098.2 0.0 reduce-scatter.5.cloned.1.call-update
  1098.3 48.1 %reduce-scatter.5.cloned.1.call-done = bf16[256,256]{1,0:T(8,128)(2,1)} async-done(((bf16[1024,256]{1,0:T(8,128)(2,1)}), bf16[256,256]{1,0:T(8,128)(2,1)}) %reduce-scatter.5.cloned.1.call-update) | async-done | bytes 131088 | tf_op jit(solution)/shard_map/reduce_scatter | solution.py:146
  (21 shorter events, 0.2 us)
Async XLA Ops:
  6.5 1087.5 %copy-start = (bf16[2048,256]{1,0:T(8,128)(2,1)S(1)}, bf16[2048,256]{1,0:T(8,128)(2,1)}, u32[]{:S(2)}) copy-start(bf16[2048,256]{1,0:T(8,128)(2,1)} %param.17) | copy-start | bytes 3145732
  6.5 7.2 copy-start.8
  6.5 159.5 %reduce-scatter.3.cloned.1.call-start = ((), (), s32[]{:S(2)}) async-start(), calls=%async_computation.2 | async-start | bytes 5406720 | tf_op jit(solution)/shard_map/reduce_scatter | solution.py:60
  13.7 882.5 %all-gather.3.cloned.1.call-start = ((), (), s32[]{:S(2)}) async-start(), calls=%async_computation.3 | async-start | bytes 34603008 | tf_op jit(solution)/shard_map/all_gather | solution.py:109
  21.0 16.0 %copy-start.11 = (s32[32]{0:T(128)S(1)}, s32[32]{0:T(128)}, u32[]{:S(2)}) copy-start(s32[32]{0:T(128)} %param.19) | copy-start | bytes 388
  21.0 18.5 %copy-start.12 = (s32[4]{0:T(128)S(1)}, s32[4]{0:T(128)}, u32[]{:S(2)}) copy-start(s32[4]{0:T(128)} %param.18) | copy-start | bytes 52
  21.0 19.1 %copy-start.2 = (bf16[1024,256]{1,0:T(8,128)(2,1)S(1)}, bf16[1024,256]{1,0:T(8,128)(2,1)}, u32[]{:S(2)}) copy-start(bf16[1024,256]{1,0:T(8,128)(2,1)} %param.11) | copy-start | bytes 1572868
  36.9 133.2 %copy-start.3 = (bf16[2,256,128]{2,1,0:T(8,128)(2,1)S(1)}, bf16[2,256,128]{2,1,0:T(8,128)(2,1)}, u32[]{:S(2)}) copy-start(bf16[2,256,128]{2,1,0:T(8,128)(2,1)} %param.14) | copy-start | bytes 393220
  36.9 1057.1 %all-gather.5.cloned.1.call-start = ((), (), s32[]{:S(2)}) async-start(), calls=%async_computation.4 | async-start | bytes 4325376 | tf_op jit(solution)/shard_map/all_gather | solution.py:142
  114.8 52.5 %copy-start.9 = (f32[32]{0:T(128)}, f32[32]{0:T(128)S(1)}, u32[]{:S(2)}) copy-start(f32[32]{0:T(128)S(1)} %add_rsqrt_fusion.1) | copy-start | bytes 388
  117.6 49.8 %copy-start.4 = (f32[32,64]{1,0:T(8,128)}, f32[32,64]{1,0:T(8,128)S(1)}, u32[]{:S(2)}) copy-start(f32[32,64]{1,0:T(8,128)S(1)} %get-tuple-element.20) | copy-start | bytes 24580
  914.6 4.8 copy-start.1
  919.5 2.5 copy-start.6
  933.5 11.4 copy-start.5
  933.6 11.4 copy-start.7
  933.6 11.4 copy-start.10
  946.1 200.3 %reduce-scatter.5.cloned.1.call-start = ((), (), s32[]{:S(2)}) async-start(), calls=%async_computation.5 | async-start | bytes 655360 | tf_op jit(solution)/shard_map/reduce_scatter | solution.py:146
Sparse Core Ops, SparseCore 0:
  13.8 152.1 reduce-scatter.2
  167.7 728.4 all-gather.2
  946.2 147.7 all-gather.4
  1098.4 47.9 reduce-scatter.4
where the time goes:
time: 1150 us
  waiting for transfers between devices  957 us (83%)
  blocking collectives  74.4 us (6%)
  matrix products  48.8 us (4%)
  other arithmetic  31.6 us (3%)
  local copies, waits for them, and re-layouts  25.6 us (2%)
  between operations  15.4 us (1%)
    all_gather x1, waiting for transfers between devices, local(): lax.all_gather(latent_pages, 'roll', axis=1, tiled=True)  721 us
    all_gather x1, waiting for transfers between devices, local(): lax.all_gather(head_values, 'roll', axis=0, tiled=True)  148 us
    psum x1, blocking collectives, local(): total_squares = lax.psum(squares, 'roll')  74.4 us
    reduce_scatter x1, waiting for transfers between devices, local(): lax.psum_scatter(partial_value.astype(jnp.bfloat16), 'tp', scatter_dimens...  48.1 us
    reduce_scatter x1, waiting for transfers between devices, local(): lax.psum_scatter(jnp.dot(scaled_rows, joined_weight, preferred_element_ty...  40.1 us
  transfers between devices with their start and end apart: 4, of which 4 were waited for; matrix products, arithmetic and copies ran while one was open for 4% of the time, Pallas kernels for 0%

commit v1 on v0

v1 whole, which is shorter than its diff:
```python
import functools

import jax
import jax.numpy as jnp
import numpy as np
from jax import lax
from jax.experimental import pallas as pl
from jax.experimental.pallas import tpu as pltpu
from jax.sharding import PartitionSpec as P

HD = 128
RANK = 256
STEPS = 4
MODEL = 8192
TOKENS = 256
PART = 1280
eps = 1e-06
rope_base = 1000000.0
SCALING = HD ** (-0.5)
NEG = -3.0e38
F32 = jnp.float32
BF16 = jnp.bfloat16
MESH_ID = pl.DeviceIdType.MESH


def rope_tables():
    freq = rope_base ** (-(np.arange(64, dtype=np.float64) * 2.0 / HD))
    freq = np.concatenate([freq, freq])

    def pair(positions):
        angles = positions[:, None] * freq[None, :]
        return np.cos(angles).astype(np.float32), np.sin(angles).astype(np.float32)

    fine = pair(np.arange(TOKENS, dtype=np.float64))
    coarse = pair(np.arange(40, dtype=np.float64) * TOKENS)
    steps = pair(np.arange(32, dtype=np.float64) % STEPS)
    return fine + coarse + steps


def rotate(values, cosine, signed_sine):
    return values * cosine + pltpu.roll(values, 64, 1) * signed_sine


def nt_dot(a, b):
    return lax.dot_general(a, b, (((1,), (1,)), ((), ())), preferred_element_type=F32)


def dot(a, b):
    return jnp.dot(a, b, preferred_element_type=F32)


def merge(outs, maxes, sums):
    top = functools.reduce(jnp.maximum, maxes)
    factors = [jnp.exp(m - top) for m in maxes]
    total = sum(f * s for f, s in zip(factors, sums))
    mixed = sum(f * o for f, o in zip(factors, outs))
    return mixed, top, total


def kernel(
    x_ref, gain_ref, wq_ref, ku_ref, vu_ref, wo_ref,
    c0_ref, s0_ref, c1_ref, s1_ref, ct_ref, st_ref,
    len_ref, gp_ref, down_hbm, ps_hbm,
    out_ref,
    slab, wd, xb, acc, sqacc, pp, r1, r2, p2, r3, p3, r4, sq, sqr,
    kb, vb, vut, qq, oo, orr, stt, sttr, o2, o2r, st2, st2r, selfo, selfs, hh, wor, ob, obr,
    loc_sem, q1s, q1r, q2s, q2r, q3s, q3r, sqs, sqrs, kvs, kvr,
    a1s, a1r, a2s, a2r, b1s, b1r, b2s, b2r, b3s, b3r, h1s, h1r, h2s, h2r, wos, worr, obs, obrr,
):
    roll = lax.axis_index("roll")
    t = lax.axis_index("tp")
    z, x, y = roll // 8, (roll // 2) % 4, roll % 2
    coord = ((z, x), (x, z))

    def dev(zz, xx, yy, tt):
        return {"roll": zz * 8 + xx * 2 + yy, "tp": tt}

    def first_dev(part, f):
        return dev(f, x, y, t) if part == 0 else dev(z, f, y, t)

    def second_dev(part, s):
        return dev(z, s, y, t) if part == 0 else dev(s, x, y, t)

    y_dev = dev(z, x, 1 - y, t)

    def remote(src, dst, ss, rs, where):
        return pltpu.make_async_remote_copy(
            src_ref=src, dst_ref=dst, send_sem=ss, recv_sem=rs, device_id=where, device_id_type=MESH_ID
        )

    def landed(dst, ss, rs):
        remote(dst, dst, ss, rs, y_dev).wait_recv()

    def sent(src, ss, rs):
        remote(src, src, ss, rs, y_dev).wait_send()

    def other(i, k):
        return (i + k) % 4

    slab_copy = pltpu.make_async_copy(
        down_hbm.at[pl.ds(pl.multiple_of(roll * 256, 256), 256)], slab, loc_sem.at[0]
    )
    slab_copy.start()
    down_copy = pltpu.make_async_copy(down_hbm, wd, loc_sem.at[1])
    down_copy.start()

    def load_prompt(p):
        return pltpu.make_async_copy(ps_hbm.at[p], xb.at[p % 2], loc_sem.at[2 + p])

    load_prompt(0).start()
    load_prompt(1).start()

    barrier = pltpu.get_barrier_semaphore()
    peers = [dev(other(z, k), x, y, t) for k in (1, 2, 3)]
    peers += [dev(z, other(x, k), y, t) for k in (1, 2, 3)]
    peers += [dev(z, x, y, other(t, k)) for k in (1, 2, 3)]
    peers += [dev(z, x, 1 - y, other(t, k)) for k in (0, 1, 2, 3)]
    for peer in peers:
        pl.semaphore_signal(barrier, inc=1, device_id=peer, device_id_type=MESH_ID)

    gain_slab = gain_ref[:, pl.ds(pl.multiple_of(roll * 256, 256), 256)].astype(F32)
    slab_copy.wait()

    def project(part, d):
        rows = x_ref[d] if part == 0 else x_ref[:, d]
        rows = (rows.reshape(256, 256).astype(F32) * gain_slab).astype(BF16)
        for c in range(4):
            got = dot(rows, wq_ref[:, part * 1024 + c * 256 : part * 1024 + (c + 1) * 256])
            pp[part, d, :, :, c * 256 : (c + 1) * 256] = got.astype(BF16).reshape(4, 64, 256)
        got = dot(rows, slab[:, part * 256 : (part + 1) * 256])
        pp[part, d, :, :, 1024:1280] = got.astype(BF16).reshape(4, 64, 256)

    def q1(part, k):
        m = coord[part][0]
        right, left = first_dev(part, other(m, 1)), first_dev(part, other(m, 3))
        lo, hi = pl.ds(0, 2), pl.ds(2, 2)
        far, near_r, near_l = other(m, 2), other(m, 1), other(m, 3)
        src, dst, where = (
            (pp.at[part, far, lo], r1.at[part, 0], right),
            (pp.at[part, far, hi], r1.at[part, 1], left),
            (pp.at[part, near_r, hi], r2.at[part, 0, hi], right),
            (pp.at[part, near_l, lo], r2.at[part, 1, lo], left),
            (pp.at[part, near_r, lo], r2.at[part, 0, lo], right),
            (pp.at[part, near_l, hi], r2.at[part, 1, hi], left),
        )[k]
        return remote(src, dst, q1s.at[part, k], q1r.at[part, k], where)

    for part in (0, 1):
        project(part, other(coord[part][0], 2))
    pl.semaphore_wait(barrier, len(peers))
    for part in (0, 1):
        q1(part, 0).start()
        q1(part, 1).start()
    for part in (0, 1):
        project(part, other(coord[part][0], 1))
        q1(part, 2).start()
    for part in (0, 1):
        project(part, other(coord[part][0], 3))
        q1(part, 3).start()
    for part in (0, 1):
        project(part, coord[part][0])

    ones = jnp.ones((8, 256), BF16)
    sub8 = lax.broadcasted_iota(jnp.int32, (8, 128), 0)
    squares = jnp.zeros((8, 128), F32)
    for i in range(8):
        rows = x_ref[i // 2, (i % 2) * 2 : (i % 2) * 2 + 2].reshape(128, 256).astype(F32)
        rows = rows * rows
        high = rows.astype(BF16)
        low = (rows - high.astype(F32)).astype(BF16)
        squares = jnp.where(sub8 == i, nt_dot(ones, high) + nt_dot(ones, low), squares)
    sq[0] = squares

    def square_copies(stage):
        if stage == 2:
            return [remote(sq.at[2], sqr.at[2, y], sqs.at[2, 1], sqrs.at[2, y], y_dev)]
        me = (z, x)[stage]
        return [
            remote(
                sq.at[stage], sqr.at[stage, me], sqs.at[stage, k], sqrs.at[stage, me],
                (dev(other(me, k), x, y, t), dev(z, other(me, k), y, t))[stage],
            )
            for k in (1, 2, 3)
        ]

    def square_sum(stage):
        total = sq[stage]
        others = [other((z, x)[stage], k) for k in (1, 2, 3)] if stage < 2 else [1 - y]
        for o in others:
            landed(sqr.at[stage, o], sqs.at[stage, 1], sqrs.at[stage, o])
            total = total + sqr[stage, o]
        return total

    for c in square_copies(0):
        c.start()

    sign = jnp.where(lax.broadcasted_iota(jnp.int32, (1, HD), 1) < 64, -1.0, 1.0)
    far_c, far_s = c1_ref[pl.ds(roll, 1), :], s1_ref[pl.ds(roll, 1), :]
    for k in (0, 1):
        vut[k] = jnp.transpose(vu_ref[k].astype(F32)).astype(BF16)

    def kv_copies(p):
        return [
            remote(b.at[y, p], b.at[y, p], kvs.at[i, p], kvr.at[i, p], y_dev)
            for i, b in enumerate((kb, vb))
        ]

    def prompt_block(p):
        load_prompt(p).wait()
        if p == 0:
            down_copy.wait()
        acc[...] = jnp.zeros_like(acc)
        sqacc[...] = jnp.zeros_like(sqacc)

        def step(i, carry):
            cols = pl.ds(pl.multiple_of(i * 1024, 1024), 1024)
            wide = xb[p % 2, :, cols].astype(F32)
            sq_wide = wide * wide
            part_sq = sq_wide[:, 0:128]
            for j in range(1, 8):
                part_sq = part_sq + sq_wide[:, j * 128 : (j + 1) * 128]
            sqacc[...] += part_sq
            scaled = (wide * gain_ref[:, cols].astype(F32)).astype(BF16)
            acc[...] += dot(scaled, wd[cols, :])
            return carry

        lax.fori_loop(0, 8, step, 0)
        if p < 2:
            load_prompt(p + 2).start()
        inverse = lax.rsqrt(jnp.sum(sqacc[...], axis=1, keepdims=True) / MODEL + eps)
        latent = (acc[...] * inverse).astype(BF16)
        cosine = far_c * c0_ref[...] - far_s * s0_ref[...]
        sine = (far_s * c0_ref[...] + far_c * s0_ref[...]) * sign
        for k in (0, 1):
            mine = latent[:, k * RANK : (k + 1) * RANK]
            kb[y, p, k] = rotate(dot(mine, ku_ref[k]), cosine, sine).astype(BF16)
            vb[y, p, k] = nt_dot(vut[k], mine).astype(BF16)
        for c in kv_copies(p):
            c.start()

    prompt_block(0)
    prompt_block(1)

    def add_into(dst, sources, blocks):
        def step(i, carry):
            rows = pl.ds(pl.multiple_of((i % 2) * 32, 32), 32)
            total = sources[0][i // 2, rows, :].astype(F32)
            for source in sources[1:]:
                total = total + source[i // 2, rows, :].astype(F32)
            dst[i // 2, rows, :] = total.astype(BF16)
            return carry

        lax.fori_loop(0, 2 * blocks, step, 0)

    for part in (0, 1):
        m = coord[part][0]
        for k, d, half in ((0, other(m, 1), 0), (1, other(m, 3), 2)):
            landed(r1.at[part, k], q1s.at[part, k], q1r.at[part, k])
            spot = pp.at[part, d, pl.ds(half, 2)]
            add_into(spot, (spot, r1.at[part, k]), 2)
            q1(part, 4 + k).start()
    sq[1] = square_sum(0)
    for c in square_copies(1):
        c.start()

    prompt_block(2)
    prompt_block(3)

    def q2(part, k):
        n = coord[part][1]
        s = other(n, k)
        return remote(p2.at[part, s], r3.at[part, n], q2s.at[part, k], q2r.at[part, n], second_dev(part, s))

    for part in (0, 1):
        m = coord[part][0]
        for k, d, half in ((2, 0, 2), (3, 1, 0), (4, 0, 0), (5, 1, 2)):
            landed(r2.at[part, d, pl.ds(half, 2)], q1s.at[part, k], q1r.at[part, k])
        add_into(p2.at[part], (pp.at[part, m], r2.at[part, 0], r2.at[part, 1]), 4)
        for k in (2, 1, 3):
            q2(part, k).start()
    sq[2] = square_sum(1)
    for c in square_copies(2):
        c.start()

    def q3(part):
        src = p3.at[part, pl.ds(pl.multiple_of((1 - y) * 32, 32), 32)]
        return remote(src, r4.at[part], q3s.at[part], q3r.at[part], y_dev)

    for part in (0, 1):
        n = coord[part][1]
        for k in (1, 3, 2):
            o = other(n, k)
            landed(r3.at[part, o], q2s.at[part, k], q2r.at[part, o])
        total = p2[part, n].astype(F32)
        for k in (1, 2, 3):
            total = total + r3[part, other(n, k)].astype(F32)
        p3[part] = total.astype(BF16)
        q3(part).start()

    prompt = gp_ref[roll]
    length = len_ref[prompt]
    hi_c, hi_s = c1_ref[pl.ds(length >> 8, 1), :], s1_ref[pl.ds(length >> 8, 1), :]
    lo_c, lo_s = c0_ref[pl.ds(length & 255, 1), :], s0_ref[pl.ds(length & 255, 1), :]
    len_c, len_s = hi_c * lo_c - hi_s * lo_s, hi_s * lo_c + hi_c * lo_s
    row_c = len_c * ct_ref[...] - len_s * st_ref[...]
    row_s = (len_s * ct_ref[...] + len_c * st_ref[...]) * sign
    all_squares = square_sum(2)
    row_squares = jnp.sum(jnp.where(sub8 == roll // 4, all_squares, 0.0), axis=0, keepdims=True)
    lane = lax.broadcasted_iota(jnp.int32, (32, 128), 1)
    sub = lax.broadcasted_iota(jnp.int32, (32, 128), 0)
    row_squares = jnp.sum(
        jnp.where(lane == (roll % 4) * 32 + sub, row_squares, 0.0), axis=1, keepdims=True
    )
    inverse = lax.rsqrt(row_squares / MODEL + eps)

    def a1(part, k):
        m, n = coord[part]
        f = other(m, k)
        return remote(qq.at[part, m, n], qq.at[part, m, n], a1s.at[part, k], a1r.at[part, m], first_dev(part, f))

    def a2(part, f, k):
        n = coord[part][1]
        return remote(
            qq.at[part, f, n], qq.at[part, f, n], a2s.at[part, f, k], a2r.at[part, f, n],
            second_dev(part, other(n, k)),
        )

    kept = []
    for part in (0, 1):
        m, n = coord[part]
        landed(r4.at[part], q3s.at[part], q3r.at[part])
        own = p3[part, pl.ds(pl.multiple_of(y * 32, 32), 32), :].astype(F32) + r4[part].astype(F32)
        own = own * inverse
        heads = [rotate(own[:, h * HD : (h + 1) * HD], row_c, row_s) for h in range(8)]
        queries = jnp.transpose(jnp.concatenate(heads, axis=0)).astype(BF16)
        qq[part, m, n] = queries
        for k in (2, 1, 3):
            a1(part, k).start()
        for k in (2, 1, 3):
            a2(part, m, k).start()
        kept.append((queries, own[:, 1024:1280].astype(BF16)))

    wo_copy = remote(wo_ref, wor, wos, worr, y_dev)
    wo_copy.start()

    key_i = lax.broadcasted_iota(jnp.int32, (32, 256), 0)
    row_i = lax.broadcasted_iota(jnp.int32, (32, 256), 1) % 32
    allowed = (key_i // STEPS == row_i // STEPS) & (key_i <= row_i)
    for part in (0, 1):
        queries, latent = kept[part]
        keys = rotate(dot(latent, ku_ref[part]), row_c, row_s).astype(BF16)
        scores = jnp.where(allowed, dot(keys, queries) * SCALING, NEG)
        top = jnp.max(scores, axis=0, keepdims=True)
        weights = jnp.exp(scores - top)
        values = nt_dot(vut[part], latent).astype(BF16)
        selfo[part] = dot(values, weights.astype(BF16))
        selfs[part, 0:1, :] = top
        selfs[part, 1:2, :] = jnp.sum(weights, axis=0, keepdims=True)

    for p in range(4):
        for i, b in enumerate((kb, vb)):
            landed(b.at[1 - y, p], kvs.at[i, p], kvr.at[i, p])
    base = (z * 4 + x) * (2 * TOKENS)
    token = lax.broadcasted_iota(jnp.int32, (TOKENS, 256), 0)

    def attend(part, f, s):
        group = (f * 8 + s * 2 if part == 0 else s * 8 + f * 2) + y
        chosen = gp_ref[group]
        limit = len_ref[chosen] - base
        queries = qq[part, f, s]
        scores = []
        for half in (0, 1):
            raw = dot(kb[half, chosen, part], queries) * SCALING
            scores.append(jnp.where(token < limit - half * TOKENS, raw, NEG))
        top = jnp.max(jnp.maximum(scores[0], scores[1]), axis=0, keepdims=True)
        weights = [jnp.exp(sc - top) for sc in scores]
        total = jnp.sum(weights[0] + weights[1], axis=0, keepdims=True)
        mixed = dot(vb[0, chosen, part], weights[0].astype(BF16))
        mixed = mixed + dot(vb[1, chosen, part], weights[1].astype(BF16))
        oo[part, f, s] = mixed.astype(BF16)
        stt[part, s, f, 0:1, :] = top
        stt[part, s, f, 1:2, :] = total

    def b1(part, f, s):
        n = coord[part][1]
        return remote(
            oo.at[part, f, s], orr.at[part, n, f], b1s.at[part, f, s], b1r.at[part, n, f], second_dev(part, s)
        )

    def b2(part, s):
        n = coord[part][1]
        return remote(stt.at[part, s], sttr.at[part, n], b2s.at[part, s], b2r.at[part, n], second_dev(part, s))

    for part in (0, 1):
        m, n = coord[part]
        for k in (1, 3, 2):
            f = other(m, k)
            landed(qq.at[part, f, n], a1s.at[part, k], a1r.at[part, f])
            for j in (2, 1, 3):
                a2(part, f, j).start()

    def own_column(i, carry):
        for part in (0, 1):
            m, n = coord[part]
            attend(part, other(m, i), n)
        return carry

    lax.fori_loop(0, 4, own_column, 0)

    def far_column(i, carry):
        for part in (0, 1):
            m, n = coord[part]
            f, s = other(m, i // 3), other(n, 1 + i % 3)
            landed(qq.at[part, f, s], a2s.at[part, 0, 0], a2r.at[part, f, s])
            attend(part, f, s)
            b1(part, f, s).start()
        return carry

    lax.fori_loop(0, 12, far_column, 0)
    for part in (0, 1):
        for k in (1, 2, 3):
            b2(part, other(coord[part][1], k)).start()

    def b3(part, f):
        m = coord[part][0]
        return (
            remote(o2.at[part, f], o2r.at[part, m], b3s.at[0, part, f], b3r.at[0, part, m], first_dev(part, f)),
            remote(st2.at[part, f], st2r.at[part, m], b3s.at[1, part, f], b3r.at[1, part, m], first_dev(part, f)),
        )

    for part in (0, 1):
        n = coord[part][1]
        for k in (1, 2, 3):
            o = other(n, k)
            landed(sttr.at[part, o], b2s.at[part, 0], b2r.at[part, o])

    def merge_column(part, f):
        n = coord[part][1]
        outs, maxes, sums = [oo[part, f, n].astype(F32)], [stt[part, n, f, 0:1, :]], [stt[part, n, f, 1:2, :]]
        for k in (1, 2, 3):
            o = other(n, k)
            landed(orr.at[part, o, f], b1s.at[part, 0, 0], b1r.at[part, o, f])
            outs.append(orr[part, o, f].astype(F32))
            maxes.append(sttr[part, o, f, 0:1, :])
            sums.append(sttr[part, o, f, 1:2, :])
        mixed, top, total = merge(outs, maxes, sums)
        o2[part, f] = mixed.astype(BF16)
        st2[part, f, 0:1, :] = top
        st2[part, f, 1:2, :] = total

    def merge_far(i, carry):
        for part in (0, 1):
            f = other(coord[part][0], i)
            merge_column(part, f)
            for c in b3(part, f):
                c.start()
        return carry

    lax.fori_loop(1, 4, merge_far, 0)
    for part in (0, 1):
        merge_column(part, coord[part][0])

    def h1(part, k):
        m, n = coord[part]
        return remote(
            hh.at[part, m, n], hh.at[part, m, n], h1s.at[part, k], h1r.at[part, m], first_dev(part, other(m, k))
        )

    def h2(part, f, k):
        n = coord[part][1]
        return remote(
            hh.at[part, f, n], hh.at[part, f, n], h2s.at[part, f, k], h2r.at[part, f, n],
            second_dev(part, other(n, k)),
        )

    for part in (0, 1):
        m, n = coord[part]
        outs = [selfo[part], o2[part, m].astype(F32)]
        maxes = [selfs[part, 0:1, :], st2[part, m, 0:1, :]]
        sums = [selfs[part, 1:2, :], st2[part, m, 1:2, :]]
        for k in (1, 3, 2):
            f = other(m, k)
            landed(o2r.at[part, f], b3s.at[0, part, 0], b3r.at[0, part, f])
            landed(st2r.at[part, f], b3s.at[1, part, 0], b3r.at[1, part, f])
            outs.append(o2r[part, f].astype(F32))
            maxes.append(st2r[part, f, 0:1, :])
            sums.append(st2r[part, f, 1:2, :])
        mixed, _, total = merge(outs, maxes, sums)
        heads = jnp.transpose(mixed / total).astype(BF16)
        for h in range(8):
            hh[part, m, n, :, h * HD : (h + 1) * HD] = heads[h * 32 : (h + 1) * 32, :]
        for k in (2, 1, 3):
            h1(part, k).start()
        for k in (2, 1, 3):
            h2(part, m, k).start()
    for part in (0, 1):
        m, n = coord[part]
        for k in (1, 3, 2):
            f = other(m, k)
            landed(hh.at[part, f, n], h1s.at[part, k], h1r.at[part, f])
            for j in (2, 1, 3):
                h2(part, f, j).start()
    wo_copy.wait_recv()
    for part in (0, 1):
        m, n = coord[part]
        for i in range(4):
            f = other(m, i)
            for k in (1, 3, 2):
                s = other(n, k)
                landed(hh.at[part, f, s], h2s.at[part, 0, 1], h2r.at[part, f, s])

    def out_block(tt):
        left = hh[0, tt].reshape(128, 1024)
        right = hh[1, :, tt].reshape(128, 1024)
        for where, weight in ((y, wo_ref), (1 - y, wor)):
            got = dot(left, weight[0:1024, :]) + dot(right, weight[1024:2048, :])
            ob[tt, where] = got.astype(BF16)

    def out_copy(tt, yy):
        return remote(ob.at[tt, yy], obr.at[t, y], obs.at[tt, yy], obrr.at[t, y], dev(z, x, yy, tt))

    for k in (2, 1, 3, 0):
        tt = other(t, k)
        out_block(tt)
        out_copy(tt, 1 - y).start()
        if k:
            out_copy(tt, y).start()
    for yy_k in (0, 1):
        yy = y if yy_k == 0 else 1 - y
        total = ob[t, y].astype(F32) if yy_k == 0 else None
        for k in ((1, 3, 2) if yy_k == 0 else (0, 1, 3, 2)):
            tt = other(t, k)
            landed(obr.at[tt, yy], obs.at[0, 0], obrr.at[tt, yy])
            piece = obr[tt, yy].astype(F32)
            total = piece if total is None else total + piece
        out_ref[:, yy] = total.astype(BF16).reshape(4, 32, 256)

    for part in (0, 1):
        m, n = coord[part]
        for k in range(6):
            q1(part, k).wait_send()
        for k in (1, 2, 3):
            q2(part, k).wait_send()
            a1(part, k).wait_send()
            h1(part, k).wait_send()
            b2(part, other(n, k)).wait_send()
            for c in b3(part, other(m, k)):
                c.wait_send()
        q3(part).wait_send()
        for i in range(4):
            for k in (1, 2, 3):
                a2(part, other(m, i), k).wait_send()
                h2(part, other(m, i), k).wait_send()
                b1(part, other(m, i), other(n, k)).wait_send()
    for stage in range(3):
        for c in square_copies(stage):
            c.wait_send()
    for p in range(4):
        for c in kv_copies(p):
            c.wait_send()
    wo_copy.wait_send()
    for k in (0, 1, 2, 3):
        out_copy(other(t, k), 1 - y).wait_send()
        if k:
            out_copy(other(t, k), y).wait_send()


def local(
    prompt_states, decode_states, norm_gain, latent_down, key_up, value_up, query_weight, out_weight,
    prompt_lengths, group_prompt,
):
    tables = [jnp.asarray(v) for v in rope_tables()]
    vmem = pl.BlockSpec(memory_space=pltpu.VMEM)
    smem = pl.BlockSpec(memory_space=pltpu.SMEM)
    hbm = pl.BlockSpec(memory_space=pl.ANY)
    V, D = pltpu.VMEM, pltpu.SemaphoreType.DMA
    scratch = [
        V((256, 512), BF16), V((MODEL, 512), BF16), V((2, TOKENS, MODEL), BF16),
        V((TOKENS, 512), F32), V((TOKENS, 128), F32),
        V((2, 4, 4, 64, PART), BF16), V((2, 2, 2, 64, PART), BF16), V((2, 2, 4, 64, PART), BF16),
        V((2, 4, 64, PART), BF16), V((2, 4, 64, PART), BF16), V((2, 64, PART), BF16), V((2, 32, PART), BF16),
        V((3, 8, 128), F32), V((3, 4, 8, 128), F32),
        V((2, 4, 2, TOKENS, HD), BF16), V((2, 4, 2, HD, TOKENS), BF16), V((2, HD, RANK), BF16),
        V((2, 4, 4, HD, 256), BF16), V((2, 4, 4, HD, 256), BF16), V((2, 4, 4, HD, 256), BF16),
        V((2, 4, 4, 8, 256), F32), V((2, 4, 4, 8, 256), F32),
        V((2, 4, HD, 256), BF16), V((2, 4, HD, 256), BF16), V((2, 4, 8, 256), F32), V((2, 4, 8, 256), F32),
        V((2, HD, 256), F32), V((2, 8, 256), F32),
        V((2, 4, 4, 32, 1024), BF16), V((2048, 256), BF16),
        V((4, 2, 128, 256), BF16), V((4, 2, 128, 256), BF16),
        D((6,)), D((2, 6)), D((2, 6)), D((2, 4)), D((2, 4)), D((2,)), D((2,)), D((3, 4)), D((3, 4)),
        D((2, 4)), D((2, 4)),
        D((2, 4)), D((2, 4)), D((2, 4, 4)), D((2, 4, 4)), D((2, 4, 4)), D((2, 4, 4)), D((2, 4)), D((2, 4)),
        D((2, 2, 4)), D((2, 2, 4)), D((2, 4)), D((2, 4)), D((2, 4, 4)), D((2, 4, 4)), D, D,
        D((4, 2)), D((4, 2)),
    ]
    out = pl.pallas_call(
        kernel,
        out_shape=jax.ShapeDtypeStruct((4, 2, 32, 256), BF16),
        in_specs=[vmem] * 12 + [smem] * 2 + [hbm] * 2,
        out_specs=vmem,
        scratch_shapes=scratch,
        compiler_params=pltpu.CompilerParams(
            collective_id=0, has_side_effects=True, vmem_limit_bytes=60 * 1024 * 1024
        ),
        cost_estimate=pl.CostEstimate(flops=16_000_000_000, bytes_accessed=30_000_000, transcendentals=5_000_000),
        name="decode_attention",
    )(
        decode_states.reshape(4, 4, 64, 256), norm_gain.reshape(1, MODEL), query_weight, key_up, value_up,
        out_weight, *tables, prompt_lengths, group_prompt, latent_down, prompt_states,
    )
    return out.reshape(256, 256)


def solution(mesh):
    return jax.shard_map(
        local,
        mesh=mesh,
        in_specs=(
            P(None, "roll", None),
            P(None, "roll"),
            P(),
            P(None, "tp"),
            P("tp", None, None),
            P("tp", None, None),
            P("roll", "tp"),
            P("tp", "roll"),
            P(),
            P(),
        ),
        out_specs=P("tp", "roll"),
        check_vma=False,
    )
```

time: 1150 us -> 113 us (0.10)
  waiting for transfers between devices: 957 us -> 0 us
  Pallas kernels: 0 us -> 110 us
  blocking collectives: 74.4 us -> 0 us
  matrix products: 48.8 us -> 0 us
  other arithmetic: 31.6 us -> 0 us
  local copies, waits for them, and re-layouts: 25.6 us -> 2.92 us
  between operations: 15.4 us -> 0.01 us
    all_gather x2 -> x0, waiting for transfers between devices: 869 us -> none  [the longest x1 721 us: local(): lax.all_gather(latent_pages, 'roll', axis=1, tiled=True)]
    pallas_call x0 -> x1, Pallas kernels: none -> 110 us  [local(): pl.pallas_call(kernel, out_shape=jax.ShapeDtypeStruct((4, 2, 32, 256), BF...]
    reduce_scatter x2 -> x0, waiting for transfers between devices: 88.2 us -> none  [the longest x1 48.1 us: local(): lax.psum_scatter(partial_value.astype(jnp.bfloat16), 'tp', scatter_dimens...]
    psum x1 -> x0, blocking collectives: 74.4 us -> none  [local(): total_squares = lax.psum(squares, 'roll')]
    dot_general x9 -> x0, matrix products: 48.8 us -> none  [the longest x1 15.9 us: local(): jnp.dot(prompt_normed, latent_down, preferred_element_type=jnp.float32)]
    dynamic_slice x6 -> x0, local copies, waits for them, and re-layouts: 21.5 us -> none  [the longest x2 18.5 us: local(): lax.dynamic_index_in_dim(lax.all_gather(latent_pages, 'roll', axis=1, til...]
    reduce_sum x4 -> x0, other arithmetic: 14.6 us -> none  [the longest x1 7.2 us: local(): jnp.mean(widened_prompts * widened_prompts, axis=-1, keepdims=True) + eps]
  transfers between devices with their start and end apart: 4 -> 0, of which waited for: 4 -> 0; matrix products, arithmetic and copies ran while one was open for 4% -> 0% of each run, Pallas kernels for 0% -> 0%
where the time goes in v1:
time: 113 us; the launch traced here: 112 us
  Pallas kernels  110 us (97%)
  local copies, waits for them, and re-layouts  2.92 us (3%)
    pallas_call x1, Pallas kernels, local(): pl.pallas_call(kernel, out_shape=jax.ShapeDtypeStruct((4, 2, 32, 256), BF...  110 us

profile of v1, /device:TPU:1, one launch (start us, length us, event | category | flops | bytes accessed | tf_op | source)
XLA Modules:
  0.0 112.4 jit_solution(6226589597418430567)
XLA Ops:
  0.0 1.3 %reshape.10.gain_ref = bf16[1,8192]{1,0:T(2,128)(2,1)} reshape(bf16[8192]{0:T(1024)(128)(2,1)} %param.18) | data formatting | bytes 32768 | tf_op jit(solution)/shard_map/reshape | solution.py:608
  1.4 109.5 %decode_attention.1 = bf16[4,2,32,256]{3,2,1,0:T(8,128)(2,1)} custom-call(bf16[4,4,64,256]{3,2,1,0:T(8,128)(2,1)} %bitcast.3, bf16[1,8192]{1,0:T(2,128)(2,1)} %reshape.10.gain_ref, bf16[256,2048]{1,0:T(8,128)(2,1)} %wq_ref.1, bf16[2,256,128]{2,1,0:T(8,128)(2,1)} %ku_ref.1, bf16[2,256,128]{2,1,0:T(8,128)(2,1)} %vu_ref.1, bf16[2048,256]{1,0:T(8,128)(2,1)} %wo_ref.1, ...), custom_call_target="tpu_custom_call" | custom-call | flops 16000000000 | bytes 30000000 | tf_op jit(solution)/shard_map/decode_attention/pallas_call | solution.py:596
  110.9 1.6 %copy.18 = bf16[256,256]{1,0:T(8,128)(2,1)} copy(bf16[256,256]{1,0:T(8,128)(2,1)} %bitcast.2) | data formatting | bytes 262144

commit v2 on v1

v2 whole, which is shorter than its diff:
```python
import functools

import jax
import jax.numpy as jnp
import numpy as np
from jax import lax
from jax.experimental import pallas as pl
from jax.experimental.pallas import tpu as pltpu
from jax.sharding import PartitionSpec as P

HD = 128
RANK = 256
STEPS = 4
MODEL = 8192
TOKENS = 256
NEAR = 1024
PAIR = 256
MIX = HD + 16
eps = 1e-06
rope_base = 1000000.0
SCALE2 = HD ** (-0.5) * float(np.log2(np.e))
NEG = -1.0e38
F32 = jnp.float32
BF16 = jnp.bfloat16
MESH_ID = pl.DeviceIdType.MESH


def rope_tables():
    freq = rope_base ** (-(np.arange(64, dtype=np.float64) * 2.0 / HD))
    freq = np.concatenate([freq, freq])

    def pair(positions):
        angles = positions[:, None] * freq[None, :]
        return np.cos(angles).astype(np.float32), np.sin(angles).astype(np.float32)

    fine = pair(np.arange(TOKENS, dtype=np.float64))
    coarse = pair(np.arange(40, dtype=np.float64) * TOKENS)
    steps = pair(np.arange(32, dtype=np.float64) % STEPS)
    return fine + coarse + steps


def rotate(values, cosine, signed_sine):
    return values * cosine + pltpu.roll(values, 64, 1) * signed_sine


def nt_dot(a, b):
    return lax.dot_general(a, b, (((1,), (1,)), ((), ())), preferred_element_type=F32)


def dot(a, b):
    return jnp.dot(a, b, preferred_element_type=F32)


def merge(outs, maxes, sums):
    top = functools.reduce(jnp.maximum, maxes)
    factors = [jnp.exp2(m - top) for m in maxes]
    total = sum(f * s for f, s in zip(factors, sums))
    mixed = sum(f * o for f, o in zip(factors, outs))
    return mixed, top, total


def terms(value):
    high = value.astype(BF16).astype(F32)
    rest = value - high
    middle = rest.astype(BF16).astype(F32)
    return [high, middle, rest - middle]


def store(ref, mixed, top, total):
    ref[0:HD] = mixed.astype(BF16)
    row = lax.broadcasted_iota(jnp.int32, (16, top.shape[1]), 0)
    tail = jnp.zeros((16, top.shape[1]), F32)
    for i, term in enumerate(terms(top) + terms(total)):
        tail = jnp.where(row == i, term, tail)
    ref[HD:MIX] = tail.astype(BF16)


def fetch(ref):
    tail = ref[HD:MIX].astype(F32)
    top = tail[0:1] + tail[1:2] + tail[2:3]
    total = tail[3:4] + tail[4:5] + tail[5:6]
    return ref[0:HD].astype(F32), top, total


def kernel(
    x_ref, gain_ref, ku_ref, vu_ref,
    c0_ref, s0_ref, c1_ref, s1_ref, ct_ref, st_ref,
    len_ref, gp_ref, wq_hbm, down_hbm, wo_hbm, ps_hbm,
    out_ref,
    gain_row, slab, wo_ref, wd, xb, acc, sqacc, xs, xo, xn, xns, wq,
    pn, pg, r1n, r1g, r2n, r2g, p2n, p2g, r3n, r3g, p3, r4, sq, sqr,
    kb, vb, vut, bias, qq, oo, orr, o2, o2r, selfo, selfs, hh, wor, ob, obc, ob2, obr,
    loc_sem, wq_sem, xws, xwr, q1s, q1r, q2s, q2r, q3s, q3r, sqs, sqrs, kvs, kvr,
    a1s, a1r, a2s, a2r, b1s, b1r, b3s, b3r, h1r, h2r, wos, worr,
    ocs, ocr, obs, obrr,
):
    roll = lax.axis_index("roll")
    t = lax.axis_index("tp")
    z, x, y = roll // 8, (roll // 2) % 4, roll % 2
    coord = ((z, x), (x, z))

    def dev(zz, xx, yy, tt):
        return {"roll": zz * 8 + xx * 2 + yy, "tp": tt}

    def first_dev(part, f):
        return dev(f, x, y, t) if part == 0 else dev(z, f, y, t)

    def second_dev(part, s):
        return dev(z, s, y, t) if part == 0 else dev(s, x, y, t)

    y_dev = dev(z, x, 1 - y, t)
    core = t % 2
    core_dev = dev(z, x, y, t + 1 - 2 * core)

    def remote(src, dst, ss, rs, where):
        return pltpu.make_async_remote_copy(
            src_ref=src, dst_ref=dst, send_sem=ss, recv_sem=rs, device_id=where, device_id_type=MESH_ID
        )

    def landed(dst, ss, rs):
        remote(dst, dst, ss, rs, y_dev).wait_recv()

    def sent(src, ss, rs):
        remote(src, src, ss, rs, y_dev).wait_send()

    def other(i, k):
        return (i + k) % 4

    slab_copy = pltpu.make_async_copy(
        down_hbm.at[pl.ds(pl.multiple_of((roll - y) * 256, 256), 512)], slab, loc_sem.at[0]
    )
    slab_copy.start()
    wq_copies = [
        pltpu.make_async_copy(wq_hbm.at[:, i * NEAR : (i + 1) * NEAR], wq.at[i], wq_sem.at[i]) for i in range(2)
    ]
    for c in wq_copies:
        c.start()
    down_copy = pltpu.make_async_copy(down_hbm, wd, loc_sem.at[1])
    down_copy.start()

    def load_prompt(p):
        return pltpu.make_async_copy(ps_hbm.at[p], xb.at[p % 2], loc_sem.at[2 + p])

    load_prompt(0).start()
    load_prompt(1).start()
    wo_load = pltpu.make_async_copy(wo_hbm, wo_ref, loc_sem.at[6])
    wo_load.start()

    barrier = pltpu.get_barrier_semaphore()
    peers = [dev(other(z, k), x, y, t) for k in (1, 2, 3)]
    peers += [dev(z, other(x, k), y, t) for k in (1, 2, 3)]
    peers += [y_dev, core_dev, dev(z, x, y, (t + 2) % 4), dev(z, x, 1 - y, (t + 2) % 4)]
    for peer in peers:
        pl.semaphore_signal(barrier, inc=1, device_id=peer, device_id_type=MESH_ID)

    streams = ((pn, r1n, r2n, p2n, r3n), (pg, r1g, r2g, p2g, r3g))

    def gain_of(owner):
        return gain_row[:, pl.ds(pl.multiple_of(owner * 256, 256), 256)]

    for i in range(8):
        gain_row[:, i * 1024 : (i + 1) * 1024] = gain_ref[i * 1024 : (i + 1) * 1024].astype(F32).reshape(1, 1024)
    own_gain = gain_of(roll)
    xo[...] = x_ref[:, :, 1 - y]
    for c in wq_copies:
        c.wait()
    for d in range(4):
        rows = x_ref[d].reshape(256, 256).astype(F32) * own_gain
        xs[d] = rows.astype(BF16).reshape(4, 2, 32, 256)

    def project_near(part, d):
        rows = (xs[d] if part == 0 else xs[:, d]).reshape(256, 256)
        for c in range(4):
            got = dot(rows, wq[part, :, c * 256 : (c + 1) * 256])
            pn[part, d, :, :, c * 256 : (c + 1) * 256] = got.astype(BF16).reshape(4, 64, 256)

    def project_pair(part, d):
        mine = (xs[d, :, y] if part == 0 else xs[:, d, y]).reshape(128, 256)
        theirs = (xns[d] if part == 0 else xns[:, d]).reshape(128, 256)
        cols = slice(part * RANK, (part + 1) * RANK)
        got = dot(mine, slab[pl.ds(pl.multiple_of(y * 256, 256), 256), cols])
        got = got + dot(theirs, slab[pl.ds(pl.multiple_of((1 - y) * 256, 256), 256), cols])
        pg[part, d] = got.astype(BF16).reshape(4, 32, 256)

    def q1(stream, part, k):
        pp, r1, r2 = streams[stream][:3]
        m = coord[part][0]
        right, left = first_dev(part, other(m, 1)), first_dev(part, other(m, 3))
        lo, hi = pl.ds(0, 2), pl.ds(2, 2)
        far, near_r, near_l = other(m, 2), other(m, 1), other(m, 3)
        src, dst, where = (
            (pp.at[part, far, lo], r1.at[part, 0], right),
            (pp.at[part, far, hi], r1.at[part, 1], left),
            (pp.at[part, near_r, hi], r2.at[part, 0, hi], right),
            (pp.at[part, near_l, lo], r2.at[part, 1, lo], left),
            (pp.at[part, near_r, lo], r2.at[part, 0, lo], right),
            (pp.at[part, near_l, hi], r2.at[part, 1, hi], left),
        )[k]
        return remote(src, dst, q1s.at[stream, part, k], q1r.at[stream, part, k], where)

    def add_into(dst, sources, blocks, per):
        def step(i, carry):
            rows = pl.ds(pl.multiple_of((i % per) * 32, 32), 32)
            total = sources[0][i // per, rows, :].astype(F32)
            for source in sources[1:]:
                total = total + source[i // per, rows, :].astype(F32)
            dst[i // per, rows, :] = total.astype(BF16)
            return carry

        lax.fori_loop(0, per * blocks, step, 0)

    def q1_forward(stream, part):
        pp, r1 = streams[stream][:2]
        m = coord[part][0]
        for k, d, half in ((0, other(m, 1), 0), (1, other(m, 3), 2)):
            landed(r1.at[part, k], q1s.at[stream, part, k], q1r.at[stream, part, k])
            spot = pp.at[part, d, pl.ds(half, 2)]
            add_into(spot, (spot, r1.at[part, k]), 2, 2 - stream)
            q1(stream, part, 4 + k).start()

    def q2(stream, part, k):
        p2, r3 = streams[stream][3:]
        n = coord[part][1]
        s = other(n, k)
        return remote(
            p2.at[part, s], r3.at[part, n], q2s.at[stream, part, k], q2r.at[stream, part, n], second_dev(part, s)
        )

    def q1_finish(stream, part):
        pp, _, r2, p2, _ = streams[stream]
        m = coord[part][0]
        for k, d, half in ((2, 0, 2), (3, 1, 0), (4, 0, 0), (5, 1, 2)):
            landed(r2.at[part, d, pl.ds(half, 2)], q1s.at[stream, part, k], q1r.at[stream, part, k])
        add_into(p2.at[part], (pp.at[part, m], r2.at[part, 0], r2.at[part, 1]), 4, 2 - stream)
        for k in (2, 1, 3):
            q2(stream, part, k).start()

    def q2_finish(stream, part):
        p2, r3 = streams[stream][3:]
        n = coord[part][1]
        for k in (1, 3, 2):
            o = other(n, k)
            landed(r3.at[part, o], q2s.at[stream, part, k], q2r.at[stream, part, o])
        total = p2[part, n].astype(F32)
        for k in (1, 2, 3):
            total = total + r3[part, other(n, k)].astype(F32)
        return total

    def q3(part):
        src = p3.at[part, pl.ds(pl.multiple_of((1 - y) * 32, 32), 32)]
        return remote(src, r4.at[part], q3s.at[part], q3r.at[part], y_dev)

    x_copy = remote(xo, xn, xws, xwr, y_dev)
    for part in (0, 1):
        project_near(part, other(coord[part][0], 2))
    pl.semaphore_wait(barrier, len(peers))
    x_copy.start()
    for part in (0, 1):
        q1(0, part, 0).start()
        q1(0, part, 1).start()
    for part in (0, 1):
        project_near(part, other(coord[part][0], 1))
        q1(0, part, 2).start()
    for part in (0, 1):
        project_near(part, other(coord[part][0], 3))
        q1(0, part, 3).start()
    for part in (0, 1):
        project_near(part, coord[part][0])
    sign = jnp.where(lax.broadcasted_iota(jnp.int32, (1, HD), 1) < 64, -1.0, 1.0)
    far_c, far_s = c1_ref[pl.ds(roll, 1), :], s1_ref[pl.ds(roll, 1), :]
    for k in (0, 1):
        vut[k] = jnp.transpose(vu_ref[k].astype(F32)).astype(BF16)

    def kv_copies(p):
        return [
            remote(b.at[y, p], b.at[y, p], kvs.at[i, p], kvr.at[i, p], y_dev)
            for i, b in enumerate((kb, vb))
        ]

    def prompt_block(p):
        load_prompt(p).wait()
        if p == 0:
            down_copy.wait()
        acc[...] = jnp.zeros_like(acc)
        sqacc[...] = jnp.zeros_like(sqacc)

        def step(i, carry):
            cols = pl.ds(pl.multiple_of(i * 1024, 1024), 1024)
            wide = xb[p % 2, :, cols].astype(F32)
            sq_wide = wide * wide
            part_sq = sq_wide[:, 0:128]
            for j in range(1, 8):
                part_sq = part_sq + sq_wide[:, j * 128 : (j + 1) * 128]
            sqacc[...] += part_sq
            scaled = (wide * gain_row[:, cols]).astype(BF16)
            acc[...] += dot(scaled, wd[cols, :])
            return carry

        lax.fori_loop(0, 8, step, 0)
        if p < 2:
            load_prompt(p + 2).start()
        inverse = lax.rsqrt(jnp.sum(sqacc[...], axis=1, keepdims=True) / MODEL + eps)
        latent = (acc[...] * inverse).astype(BF16)
        cosine = far_c * c0_ref[...] - far_s * s0_ref[...]
        sine = (far_s * c0_ref[...] + far_c * s0_ref[...]) * sign
        for k in (0, 1):
            mine = latent[:, k * RANK : (k + 1) * RANK]
            kb[y, p, k] = rotate(dot(mine, ku_ref[k]), cosine, sine).astype(BF16)
            vb[y, p, k] = nt_dot(vut[k], mine).astype(BF16)

    def send_kv(p):
        for c in kv_copies(p):
            c.start()

    prompt_block(0)
    slab_copy.wait()
    x_copy.wait_recv()
    sub8 = lax.broadcasted_iota(jnp.int32, (8, 128), 0)
    diagonal = lax.broadcasted_iota(jnp.int32, (128, 128), 0) == lax.broadcasted_iota(jnp.int32, (128, 128), 1)
    their_gain = gain_of(roll + 1 - 2 * y)
    squares = jnp.zeros((8, 128), F32)
    for d in range(4):
        mine = x_ref[d, :, y].reshape(128, 256).astype(F32)
        theirs = xn[d].reshape(128, 256).astype(F32)
        xns[d] = (theirs * their_gain).astype(BF16).reshape(4, 32, 256)
        total = jnp.sum(mine * mine + theirs * theirs, axis=1, keepdims=True)
        as_row = jnp.sum(jnp.where(diagonal, total, 0.0), axis=0, keepdims=True)
        squares = jnp.where(sub8 == d, as_row, squares)
    sq[0] = squares

    def square_copies(stage):
        me = (z, x)[stage]
        return [
            remote(
                sq.at[stage], sqr.at[stage, me], sqs.at[stage, k], sqrs.at[stage, me],
                (dev(other(me, k), x, y, t), dev(z, other(me, k), y, t))[stage],
            )
            for k in (1, 2, 3)
        ]

    def square_sum(stage):
        total = sq[stage]
        for k in (1, 2, 3):
            o = other((z, x)[stage], k)
            landed(sqr.at[stage, o], sqs.at[stage, 1], sqrs.at[stage, o])
            total = total + sqr[stage, o]
        return total

    for c in square_copies(0):
        c.start()
    for part in (0, 1):
        for k in (2, 1, 3, 0):
            project_pair(part, other(coord[part][0], k))
            for i in {2: (0, 1), 1: (2,), 3: (3,), 0: ()}[k]:
                q1(1, part, i).start()
    send_kv(0)
    for part in (0, 1):
        q1_forward(0, part)
    prompt_block(1)
    send_kv(1)
    for part in (0, 1):
        q1_forward(1, part)
    sq[1] = square_sum(0)
    for c in square_copies(1):
        c.start()
    prompt_block(2)
    send_kv(2)
    for part in (0, 1):
        q1_finish(0, part)
    for part in (0, 1):
        q1_finish(1, part)
    prompt_block(3)
    send_kv(3)
    for part in (0, 1):
        p3[part] = q2_finish(0, part).astype(BF16)
        q3(part).start()

    prompt = gp_ref[roll]
    length = len_ref[prompt]
    hi_c, hi_s = c1_ref[pl.ds(length >> 8, 1), :], s1_ref[pl.ds(length >> 8, 1), :]
    lo_c, lo_s = c0_ref[pl.ds(length & 255, 1), :], s0_ref[pl.ds(length & 255, 1), :]
    len_c, len_s = hi_c * lo_c - hi_s * lo_s, hi_s * lo_c + hi_c * lo_s
    row_c = len_c * ct_ref[...] - len_s * st_ref[...]
    row_s = (len_s * ct_ref[...] + len_c * st_ref[...]) * sign
    all_squares = square_sum(1)
    row_squares = jnp.sum(jnp.where(sub8 == z, all_squares, 0.0), axis=0, keepdims=True)
    lane = lax.broadcasted_iota(jnp.int32, (32, 128), 1)
    sub = lax.broadcasted_iota(jnp.int32, (32, 128), 0)
    row_squares = jnp.sum(
        jnp.where(lane == x * 32 + sub, row_squares, 0.0), axis=1, keepdims=True
    )
    inverse = lax.rsqrt(row_squares / MODEL + eps)

    def a1(part, k):
        m, n = coord[part]
        f = other(m, k)
        return remote(qq.at[part, m, n], qq.at[part, m, n], a1s.at[part, k], a1r.at[part, m], first_dev(part, f))

    def ring(buf, half, send, recv, part, f, k):
        n = coord[part][1]
        spot = buf.at[part, f, (n, n, other(n, 3), other(n, 1))[k]]
        if k >= 2:
            spot = spot.at[pl.ds((k - 2) * half, half)]
        to = second_dev(part, other(n, (1, 3)[k % 2]))
        return remote(spot, spot, send.at[part, f, k], recv.at[part, f, k], to)

    def ring_near(buf, half, send, recv, part, f):
        n = coord[part][1]
        for k in (0, 1):
            landed(buf.at[part, f, other(n, (3, 1)[k])], send.at[part, f, k], recv.at[part, f, k])
            ring(buf, half, send, recv, part, f, 2 + k).start()

    def ring_far(buf, half, send, recv, part, f):
        spot = buf.at[part, f, other(coord[part][1], 2)]
        for k in (2, 3):
            landed(spot.at[pl.ds((k - 2) * half, half)], send.at[part, f, k], recv.at[part, f, k])

    q_ring = (qq, 64, a2s, a2r)
    h_ring = (hh, 16, a2s, h2r)

    kept = []
    for part in (0, 1):
        m, n = coord[part]
        landed(r4.at[part], q3s.at[part], q3r.at[part])
        near = p3[part, pl.ds(pl.multiple_of(y * 32, 32), 32), :].astype(F32) + r4[part].astype(F32)
        near = near * inverse
        pair = q2_finish(1, part) * inverse
        heads = [rotate(near[:, h * HD : (h + 1) * HD], row_c, row_s) for h in range(8)]
        queries = jnp.transpose(jnp.concatenate(heads, axis=0)).astype(BF16)
        qq[part, m, n] = queries
        for k in (2, 1, 3):
            a1(part, k).start()
        for k in (0, 1):
            ring(*q_ring, part, m, k).start()
        kept.append((queries, pair.astype(BF16)))

    wo_copy = remote(wo_ref, wor, wos, worr, y_dev)
    wo_load.wait()
    wo_copy.start()

    key_i = lax.broadcasted_iota(jnp.int32, (32, 256), 0)
    row_i = lax.broadcasted_iota(jnp.int32, (32, 256), 1) % 32
    allowed = (key_i // STEPS == row_i // STEPS) & (key_i <= row_i)
    for part in (0, 1):
        queries, latent = kept[part]
        keys = rotate(dot(latent, ku_ref[part]), row_c, row_s).astype(BF16)
        scores = jnp.where(allowed, dot(keys, queries) * SCALE2, NEG)
        top = jnp.max(scores, axis=0, keepdims=True)
        weights = jnp.exp2(scores - top)
        values = nt_dot(vut[part], latent).astype(BF16)
        selfo[part] = dot(values, weights.astype(BF16))
        selfs[part, 0:1, :] = top
        selfs[part, 1:2, :] = jnp.sum(weights, axis=0, keepdims=True)

    for p in range(4):
        for i, b in enumerate((kb, vb)):
            landed(b.at[1 - y, p], kvs.at[i, p], kvr.at[i, p])
    base = (z * 4 + x) * (2 * TOKENS)

    token = lax.broadcasted_iota(jnp.int32, (TOKENS, HD), 0)
    first = lax.broadcasted_iota(jnp.int32, (TOKENS, HD), 1) == 0
    for p in range(4):
        for half in (0, 1):
            past = token >= len_ref[p] - base - half * TOKENS
            bias[p, half] = jnp.where(first & past, NEG, 0.0).astype(BF16)
    ones_row = jnp.where(lax.broadcasted_iota(jnp.int32, (HD, 256), 0) == 0, 1.0, 0.0).astype(BF16)
    ones_tail = jnp.ones((16, TOKENS), BF16)

    def attend(part, f, s):
        group = (f * 8 + s * 2 if part == 0 else s * 8 + f * 2) + y
        chosen = gp_ref[group]
        queries = jnp.concatenate([qq[part, f, s], ones_row], axis=0)
        scores = [
            dot(jnp.concatenate([kb[half, chosen, part], bias[chosen, half]], axis=1), queries)
            for half in (0, 1)
        ]
        top = jnp.max(jnp.maximum(scores[0], scores[1]), axis=0, keepdims=True)
        shift = top * SCALE2
        weights = [jnp.exp2(sc * SCALE2 - shift).astype(BF16) for sc in scores]
        mixed = dot(jnp.concatenate([vb[0, chosen, part], ones_tail], axis=0), weights[0])
        mixed = mixed + dot(jnp.concatenate([vb[1, chosen, part], ones_tail], axis=0), weights[1])
        store(oo.at[part, f, s], mixed[0:HD], shift, mixed[HD : HD + 1])

    def b1(part, f, s):
        n = coord[part][1]
        return remote(
            oo.at[part, f, s], orr.at[part, n, f], b1s.at[part, f, s], b1r.at[part, n, f], second_dev(part, s)
        )

    def b3(part, f):
        m = coord[part][0]
        return remote(o2.at[part, f], o2r.at[part, m], b3s.at[part, f], b3r.at[part, m], first_dev(part, f))

    for part in (0, 1):
        m, n = coord[part]
        for k in (1, 3, 2):
            f = other(m, k)
            landed(qq.at[part, f, n], a1s.at[part, k], a1r.at[part, f])
            for j in (0, 1):
                ring(*q_ring, part, f, j).start()

    def own_column(i, carry):
        for part in (0, 1):
            m, n = coord[part]
            attend(part, other(m, i), n)
        return carry

    lax.fori_loop(0, 4, own_column, 0)

    def forward(i):
        for part in (0, 1):
            ring_near(*q_ring, part, other(coord[part][0], i))

    def answer(part, i, k):
        m, n = coord[part]
        f, s = other(m, i), other(n, k)
        attend(part, f, s)
        b1(part, f, s).start()

    def near_columns(i):
        def step(j, carry):
            for part in (0, 1):
                answer(part, i, 1 + 2 * j)
            return carry

        lax.fori_loop(0, 2, step, 0)

    def far_column(i):
        for part in (0, 1):
            ring_far(*q_ring, part, other(coord[part][0], i))
            answer(part, i, 2)

    def merge_column(part, f):
        n = coord[part][1]
        found = [fetch(oo.at[part, f, n])]
        for k in (1, 3, 2):
            o = other(n, k)
            landed(orr.at[part, o, f], b1s.at[part, 0, 0], b1r.at[part, o, f])
            found.append(fetch(orr.at[part, o, f]))
        store(o2.at[part, f], *merge(*zip(*found)))

    def merge_columns(i):
        for part in (0, 1):
            f = other(coord[part][0], i)
            merge_column(part, f)
            if i:
                b3(part, f).start()

    forward(0)
    forward(1)
    near_columns(1)
    forward(2)
    far_column(1)
    near_columns(2)
    forward(3)
    far_column(2)
    near_columns(3)
    merge_columns(1)
    near_columns(0)
    far_column(3)
    merge_columns(2)
    far_column(0)
    merge_columns(3)
    merge_columns(0)

    for part in (0, 1):
        for k in (1, 2, 3):
            a1(part, k).wait_send()
        for f in range(4):
            for k in range(4):
                ring(*q_ring, part, f, k).wait_send()

    def h1(part, k):
        m, n = coord[part]
        return remote(
            hh.at[part, m, n], hh.at[part, m, n], a1s.at[part, k], h1r.at[part, m], first_dev(part, other(m, k))
        )

    for part in (0, 1):
        m, n = coord[part]
        found = [(selfo[part], selfs[part, 0:1, :], selfs[part, 1:2, :]), fetch(o2.at[part, m])]
        for k in (1, 3, 2):
            f = other(m, k)
            landed(o2r.at[part, f], b3s.at[part, 0], b3r.at[part, f])
            found.append(fetch(o2r.at[part, f]))
        mixed, _, total = merge(*zip(*found))
        heads = jnp.transpose(mixed / total).astype(BF16)
        for h in range(8):
            hh[part, m, n, :, h * HD : (h + 1) * HD] = heads[h * 32 : (h + 1) * 32, :]
        for k in (2, 1, 3):
            h1(part, k).start()
        for k in (0, 1):
            ring(*h_ring, part, m, k).start()
    for part in (0, 1):
        m, n = coord[part]
        for k in (1, 3, 2):
            f = other(m, k)
            landed(hh.at[part, f, n], a1s.at[part, k], h1r.at[part, f])
            for j in (0, 1):
                ring(*h_ring, part, f, j).start()
    for i in (0, 3, 1, 2):
        for part in (0, 1):
            ring_near(*h_ring, part, other(coord[part][0], i))
    wo_copy.wait_recv()

    def out_block(tt):
        left = hh[0, tt].reshape(128, 1024)
        right = hh[1, :, tt].reshape(128, 1024)
        for where, weight in ((y, wo_ref), (1 - y, wor)):
            got = dot(left, weight[0:1024, :]) + dot(right, weight[1024:2048, :])
            ob[tt, where] = got.astype(BF16)

    def core_copy(tt):
        return remote(ob.at[tt], obc.at[tt // 2], ocs.at[tt // 2], ocr.at[tt // 2], core_dev)

    def chip_copy(half, yy):
        return remote(
            ob2.at[half, yy], obr.at[t // 2, y], obs.at[half, yy], obrr.at[t // 2, y],
            dev(z, x, yy, half * 2 + core),
        )

    for k in (0, 3, 1, 2):
        tt = other(z, k)
        ring_far(*h_ring, 0, tt)
        if k == 2:
            for f in range(4):
                ring_far(*h_ring, 1, f)
        out_block(tt)
        half = tt // 2

        @pl.when(tt % 2 != core)
        def _():
            core_copy(tt).start()

        @pl.when(tt % 2 == core)
        def _():
            landed(obc.at[half], ocs.at[0], ocr.at[half])
            ob2[half] = (ob[tt].astype(F32) + obc[half].astype(F32)).astype(BF16)
            chip_copy(half, 1 - y).start()

            @pl.when(half != t // 2)
            def _():
                chip_copy(half, y).start()

    here = t // 2
    for yy_k in (0, 1):
        yy = y if yy_k == 0 else 1 - y
        landed(obr.at[1 - here, yy], obs.at[0, 0], obrr.at[1 - here, yy])
        total = obr[1 - here, yy].astype(F32)
        if yy_k == 0:
            total = total + ob2[here, y].astype(F32)
        else:
            landed(obr.at[here, yy], obs.at[0, 0], obrr.at[here, yy])
            total = total + obr[here, yy].astype(F32)
        out_ref[:, yy] = total.astype(BF16).reshape(4, 32, 256)

    for part in (0, 1):
        m, n = coord[part]
        for stream in (0, 1):
            for k in range(6):
                q1(stream, part, k).wait_send()
            for k in (1, 2, 3):
                q2(stream, part, k).wait_send()
        for k in (1, 2, 3):
            h1(part, k).wait_send()
            b3(part, other(m, k)).wait_send()
        q3(part).wait_send()
        for i in range(4):
            for k in (1, 2, 3):
                b1(part, other(m, i), other(n, k)).wait_send()
            for k in range(4):
                ring(*h_ring, part, i, k).wait_send()
    for stage in range(2):
        for c in square_copies(stage):
            c.wait_send()
    for p in range(4):
        for c in kv_copies(p):
            c.wait_send()
    wo_copy.wait_send()
    x_copy.wait_send()
    for half in (0, 1):
        core_copy(2 * half + 1 - core).wait_send()
        chip_copy(half, 1 - y).wait_send()
    chip_copy(1 - here, y).wait_send()


def local(
    prompt_states, decode_states, norm_gain, latent_down, key_up, value_up, query_weight, out_weight,
    prompt_lengths, group_prompt,
):
    tables = [jnp.asarray(v) for v in rope_tables()]
    vmem = pl.BlockSpec(memory_space=pltpu.VMEM)
    smem = pl.BlockSpec(memory_space=pltpu.SMEM)
    hbm = pl.BlockSpec(memory_space=pl.ANY)
    V, D = pltpu.VMEM, pltpu.SemaphoreType.DMA
    scratch = [
        V((1, MODEL), F32), V((512, 512), BF16), V((2048, 256), BF16), V((MODEL, 512), BF16), V((2, TOKENS, MODEL), BF16),
        V((TOKENS, 512), F32), V((TOKENS, 128), F32),
        V((4, 4, 2, 32, 256), BF16), V((4, 4, 32, 256), BF16), V((4, 4, 32, 256), BF16), V((4, 4, 32, 256), BF16),
        V((2, 256, NEAR), BF16),
        V((2, 4, 4, 64, NEAR), BF16), V((2, 4, 4, 32, PAIR), BF16),
        V((2, 2, 2, 64, NEAR), BF16), V((2, 2, 2, 32, PAIR), BF16),
        V((2, 2, 4, 64, NEAR), BF16), V((2, 2, 4, 32, PAIR), BF16),
        V((2, 4, 64, NEAR), BF16), V((2, 4, 32, PAIR), BF16),
        V((2, 4, 64, NEAR), BF16), V((2, 4, 32, PAIR), BF16),
        V((2, 64, NEAR), BF16), V((2, 32, NEAR), BF16),
        V((2, 8, 128), F32), V((2, 4, 8, 128), F32),
        V((2, 4, 2, TOKENS, HD), BF16), V((2, 4, 2, HD, TOKENS), BF16), V((2, HD, RANK), BF16),
        V((4, 2, TOKENS, HD), BF16),
        V((2, 4, 4, HD, 256), BF16), V((2, 4, 4, MIX, 256), BF16), V((2, 4, 4, MIX, 256), BF16),
        V((2, 4, MIX, 256), BF16), V((2, 4, MIX, 256), BF16),
        V((2, HD, 256), F32), V((2, 8, 256), F32),
        V((2, 4, 4, 32, 1024), BF16), V((2048, 256), BF16),
        V((4, 2, 128, 256), BF16), V((2, 2, 128, 256), BF16), V((2, 2, 128, 256), BF16), V((2, 2, 128, 256), BF16),
        D((7,)), D((2,)), D, D, D((2, 2, 6)), D((2, 2, 6)), D((2, 2, 4)), D((2, 2, 4)), D((2,)), D((2,)),
        D((2, 4)), D((2, 4)),
        D((2, 4)), D((2, 4)),
        D((2, 4)), D((2, 4)), D((2, 4, 4)), D((2, 4, 4)), D((2, 4, 4)), D((2, 4, 4)),
        D((2, 4)), D((2, 4)), D((2, 4)), D((2, 4, 4)), D, D,
        D((2,)), D((2,)), D((2, 2)), D((2, 2)),
    ]
    out = pl.pallas_call(
        kernel,
        out_shape=jax.ShapeDtypeStruct((4, 2, 32, 256), BF16),
        in_specs=[vmem] * 10 + [smem] * 2 + [hbm] * 4,
        out_specs=vmem,
        scratch_shapes=scratch,
        compiler_params=pltpu.CompilerParams(
            collective_id=0, has_side_effects=True, vmem_limit_bytes=60 * 1024 * 1024
        ),
        cost_estimate=pl.CostEstimate(flops=16_000_000_000, bytes_accessed=30_000_000, transcendentals=5_000_000),
        name="decode_attention",
    )(
        decode_states.reshape(4, 4, 2, 32, 256), norm_gain, key_up, value_up,
        *tables, prompt_lengths, group_prompt, query_weight, latent_down, out_weight,
        prompt_states,
    )
    return out.reshape(256, 256)


def solution(mesh):
    return jax.shard_map(
        local,
        mesh=mesh,
        in_specs=(
            P(None, "roll", None),
            P(None, "roll"),
            P(),
            P(None, "tp"),
            P("tp", None, None),
            P("tp", None, None),
            P("roll", "tp"),
            P("tp", "roll"),
            P(),
            P(),
        ),
        out_specs=P("tp", "roll"),
        check_vma=False,
    )
```

time: 113 us -> 109 us (0.965)
  Pallas kernels: 110 us -> 107 us
  local copies, waits for them, and re-layouts: 2.92 us -> 1.57 us
    pallas_call x1, Pallas kernels: 110 us -> 107 us  [local(): pl.pallas_call(kernel, out_shape=jax.ShapeDtypeStruct((4, 2, 32, 256), BF...]
    reshape x1 -> x0, local copies, waits for them, and re-layouts: 1.35 us -> none  [local(): norm_gain.reshape(1, MODEL)]
where the time goes in v2:
time: 109 us; the launch traced here: 108 us
  Pallas kernels  107 us (98%)
  local copies, waits for them, and re-layouts  1.57 us (1%)
    pallas_call x1, Pallas kernels, local(): pl.pallas_call(kernel, out_shape=jax.ShapeDtypeStruct((4, 2, 32, 256), BF...  107 us

profile of v2, /device:TPU:1, one launch (start us, length us, event | category | flops | bytes accessed | tf_op | source)
XLA Modules:
  0.0 108.5 jit_solution(4284078411532595278)
XLA Ops:
  0.0 106.9 %decode_attention.1 = bf16[4,2,32,256]{3,2,1,0:T(8,128)(2,1)} custom-call(bf16[4,4,2,32,256]{4,3,2,1,0:T(8,128)(2,1)} %bitcast.3, bf16[8192]{0:T(1024)(128)(2,1)} %gain_ref.1, bf16[2,256,128]{2,1,0:T(8,128)(2,1)} %ku_ref.1, bf16[2,256,128]{2,1,0:T(8,128)(2,1)} %vu_ref.1, f32[256,128]{1,0:T(8,128)} %constant.12.clone.c0_ref, ...), custom_call_target="tpu_custom_call" | custom-call | flops 16000000000 | bytes 30000000 | tf_op jit(solution)/shard_map/decode_attention/pallas_call | solution.py:722
  106.9 1.6 %copy.18 = bf16[256,256]{1,0:T(8,128)(2,1)} copy(bf16[256,256]{1,0:T(8,128)(2,1)} %bitcast.2) | data formatting | bytes 262144

commit v3 on v2

--- a/solution.py
+++ b/solution.py
@@ -370,7 +370,6 @@
     for part in (0, 1):
         q1_finish(1, part)
     prompt_block(3)
-    send_kv(3)
     for part in (0, 1):
         p3[part] = q2_finish(0, part).astype(BF16)
         q3(part).start()
@@ -436,7 +435,7 @@
 
     wo_copy = remote(wo_ref, wor, wos, worr, y_dev)
     wo_load.wait()
-    wo_copy.start()
+    send_kv(3)
 
     key_i = lax.broadcasted_iota(jnp.int32, (32, 256), 0)
     row_i = lax.broadcasted_iota(jnp.int32, (32, 256), 1) % 32
@@ -455,6 +454,7 @@
     for p in range(4):
         for i, b in enumerate((kb, vb)):
             landed(b.at[1 - y, p], kvs.at[i, p], kvr.at[i, p])
+    wo_copy.start()
     base = (z * 4 + x) * (2 * TOKENS)
 
     token = lax.broadcasted_iota(jnp.int32, (TOKENS, HD), 0)

time: 109 us -> 107 us (0.982)
  Pallas kernels: 107 us -> 105 us
    pallas_call x1, Pallas kernels: 107 us -> 105 us  [local(): pl.pallas_call(kernel, out_shape=jax.ShapeDtypeStruct((4, 2, 32, 256), BF...]
where the time goes in v3:
time: 107 us; the launch traced here: 106 us
  Pallas kernels  105 us (98%)
  local copies, waits for them, and re-layouts  1.57 us (1%)
    pallas_call x1, Pallas kernels, local(): pl.pallas_call(kernel, out_shape=jax.ShapeDtypeStruct((4, 2, 32, 256), BF...  105 us

profile of v3, /device:TPU:1, one launch (start us, length us, event | category | flops | bytes accessed | tf_op | source)
XLA Modules:
  0.0 106.5 jit_solution(17150596252785666362)
XLA Ops:
  0.0 104.9 %decode_attention.1 = bf16[4,2,32,256]{3,2,1,0:T(8,128)(2,1)} custom-call(bf16[4,4,2,32,256]{4,3,2,1,0:T(8,128)(2,1)} %bitcast.3, bf16[8192]{0:T(1024)(128)(2,1)} %gain_ref.1, bf16[2,256,128]{2,1,0:T(8,128)(2,1)} %ku_ref.1, bf16[2,256,128]{2,1,0:T(8,128)(2,1)} %vu_ref.1, f32[256,128]{1,0:T(8,128)} %constant.12.clone.c0_ref, ...), custom_call_target="tpu_custom_call" | custom-call | flops 16000000000 | bytes 30000000 | tf_op jit(solution)/shard_map/decode_attention/pallas_call | solution.py:722
  104.9 1.6 %copy.18 = bf16[256,256]{1,0:T(8,128)(2,1)} copy(bf16[256,256]{1,0:T(8,128)(2,1)} %bitcast.2) | data formatting | bytes 262144
